TPU v7x, 32 devices: a whole 2x2x4 slice. The times are simulated.
32 devices in a mesh: groups: 2 (over x), tiles: 16 (over z, y, core).
Axes of the slice: x: 2, y: 2, z: 4, core: 2. Of those that a mesh axis runs over, the one named last changes fastest.
Arguments:
- tiles: bfloat16 [4096, 1536], P(('groups', 'tiles')), parts along dimension 0, may hold values from -6 to 6
- tile_region: int32 [4096, 1], P(('groups', 'tiles')), parts along dimension 0, may hold values from 0 to 15; in each aligned block of 128 rows (0 to 127, 128 to 255, ...) at most 16 rows name the same one
- slide_of_region: int32 [32], P('groups'), parts along dimension 0, may hold values from 0 to 1, never falling along the last dimension, each value on 1 to 12 neighbouring positions
- seg_offset: int32 [12], replicated, may hold values from 0 to 3
- w_in: bfloat16 [1536, 384], replicated, may hold values from -0.15625 to 0.15625
- w_qkv: bfloat16 [384, 1152], replicated, may hold values from -1 to 1
- w_attn_out: bfloat16 [384, 384], replicated, may hold values from -0.3125 to 0.3125
- w_up: bfloat16 [384, 1536], replicated, may hold values from -0.3125 to 0.3125
- w_down: bfloat16 [1536, 384], replicated, may hold values from -0.15625 to 0.15625
- w_slide_in: bfloat16 [384, 768], replicated, may hold values from -0.3125 to 0.3125
- w_slide_qkv: bfloat16 [768, 2304], replicated, may hold values from -1 to 1
- w_slide_out: bfloat16 [768, 768], replicated, may hold values from -0.21875 to 0.21875
- slide_ct: bfloat16 [32, 768], P(('groups', 'tiles')), parts along dimension 0, may hold values from -6 to 6
Outputs:
- slide_out: bfloat16 [32, 768], P(('groups', 'tiles')), parts along dimension 0
- tile_grad: bfloat16 [4096, 1536], P(('groups', 'tiles')), parts along dimension 0
There are 2 independent parts, one for each index of `groups`. A program takes and returns all parts, laid end to end along the dimension named above; an argument that names none is the same for every part. Nothing has to cross between parts.
Inputs may be any that keep to these rules, and one draw needn't show every extreme that they name: `tile_region`: each tile names one region; the tiles of one device name one region at most 16 times, and exactly 16 times for some region in every draw; every region is named by some tile. `slide_of_region`: never falling along the regions.
All inputs are finite; a program needn't handle non-finite values.
Results may differ from a plain program's by a relative error of at most 0.03.
Values may be sent and summed in bfloat16 or wider, within the bound.
A program may use at most 64 MiB of HBM per device.

v0:
```python
import jax
import jax.numpy as jnp
from jax import lax
from jax.sharding import PartitionSpec as P

HEADS_R = 6
HEADS_S = 12
REGION_SLOTS = 256
DILATION = 4


def layer_norm(values):
    average = jnp.mean(values, axis=-1, keepdims=True)
    centred = values - average
    variance = jnp.mean(centred * centred, axis=-1, keepdims=True)
    return centred * lax.rsqrt(variance + 1e-05)


def rounded(values):
    return lax.optimization_barrier(values.astype(jnp.bfloat16)).astype(jnp.float32)


def masked_softmax(scores, allowed):
    scores = jnp.where(allowed, scores, -1e30)
    highest = jnp.max(scores, axis=-1, keepdims=True)
    raised = jnp.exp(scores - highest)
    return rounded(raised / jnp.sum(raised, axis=-1, keepdims=True))


def region_layers(hidden, filled, w_qkv, w_attn_out, w_up, w_down, head_count):
    groups, length, width = hidden.shape
    head_size = width // head_count
    normed = layer_norm(hidden).astype(jnp.bfloat16).reshape(groups * length, width)
    packed = rounded(jnp.dot(normed, w_qkv, preferred_element_type=jnp.float32))
    packed = packed.reshape(groups, length, 3, head_count, head_size)
    queries = packed[:, :, 0]
    keys_part = packed[:, :, 1]
    values_part = packed[:, :, 2]
    scores = jnp.einsum("gqhd,gkhd->ghqk", queries, keys_part) * head_size ** (-0.5)
    attention = masked_softmax(scores, (filled > 0)[:, None, None, :])
    mixed = jnp.einsum("ghqk,gkhd->gqhd", attention, values_part)
    mixed = mixed.astype(jnp.bfloat16).reshape(groups * length, width)
    first = hidden + jnp.dot(mixed, w_attn_out, preferred_element_type=jnp.float32).reshape(
        groups, length, width
    )
    normed_two = layer_norm(first).astype(jnp.bfloat16).reshape(groups * length, width)
    inner = jax.nn.gelu(jnp.dot(normed_two, w_up, preferred_element_type=jnp.float32)).astype(
        jnp.bfloat16
    )
    second = first + jnp.dot(inner, w_down, preferred_element_type=jnp.float32).reshape(
        groups, length, width
    )
    counted = jnp.sum(filled, axis=1)
    return jnp.sum(second * filled[:, :, None], axis=1) / counted[:, None]


def slide_front(pooled, w_slide_in, w_slide_qkv):
    width = w_slide_in.shape[1]
    token_rows = jnp.dot(
        layer_norm(pooled).astype(jnp.bfloat16), w_slide_in, preferred_element_type=jnp.float32
    )
    packed = jnp.dot(
        layer_norm(token_rows).astype(jnp.bfloat16), w_slide_qkv, preferred_element_type=jnp.float32
    )
    packed = packed.astype(jnp.bfloat16)
    return (token_rows, packed[:, :width], packed[:, width:])


def slide_mix(
    token_rows,
    queries,
    key_values,
    query_index,
    query_slide,
    slide_of_region,
    seg_offset,
    w_slide_out,
    head_count,
):
    rows, width = token_rows.shape
    head_size = width // head_count
    count = key_values.shape[0]
    query_heads = queries.astype(jnp.float32).reshape(rows, head_count, head_size)
    keys_part = key_values[:, :width].reshape(count, head_count, head_size)
    values_part = key_values[:, width:].reshape(count, head_count, head_size)
    scores = jnp.einsum("qhd,khd->hqk", query_heads, keys_part) * head_size ** (-0.5)
    key_index = jnp.arange(count, dtype=jnp.int32)
    same_slide = query_slide[:, None] == slide_of_region[None, :]
    dilated = (key_index[None, :] + seg_offset[:, None]) % DILATION == 0
    itself = query_index[:, None] == key_index[None, :]
    allowed = same_slide[None] & (dilated[:, None, :] | itself[None])
    attention = masked_softmax(scores, allowed)
    mixed = (
        jnp.einsum("hqk,khd->qhd", attention, values_part).astype(jnp.bfloat16).reshape(rows, width)
    )
    return (token_rows + jnp.dot(mixed, w_slide_out, preferred_element_type=jnp.float32)).astype(
        jnp.bfloat16
    )


def local(
    tiles,
    tile_region,
    slide_of_region,
    seg_offset,
    w_in,
    w_qkv,
    w_attn_out,
    w_up,
    w_down,
    w_slide_in,
    w_slide_qkv,
    w_slide_out,
    slide_ct,
):
    devices = lax.axis_size("tiles")
    position = lax.axis_index("tiles")
    own_regions = slide_ct.shape[0]
    capacity = REGION_SLOTS // devices
    region_total = own_regions * devices
    slots_all = own_regions * devices * capacity
    layout = (own_regions, devices, capacity)
    region = tile_region[:, 0]
    onehot = (region[:, None] == jnp.arange(region_total, dtype=jnp.int32)[None, :]).astype(
        jnp.int32
    )
    before = jnp.cumsum(onehot, axis=0) - onehot
    rank = jnp.sum(before * onehot, axis=1)
    owner = region // own_regions
    target = region % own_regions * (devices * capacity) + owner * capacity + rank

    def project_rows(rows):
        return jnp.dot(rows, w_in, preferred_element_type=jnp.float32)

    outgoing = jnp.zeros((slots_all, tiles.shape[1]), jnp.bfloat16).at[target].set(tiles)
    marks = jnp.zeros((slots_all,), jnp.bfloat16).at[target].set(1.0)
    arrived, arrived_marks = (
        lax.all_to_all(
            outgoing.reshape(layout + (tiles.shape[1],)),
            "tiles",
            split_axis=1,
            concat_axis=1,
            tiled=True,
        ),
        lax.all_to_all(marks.reshape(layout), "tiles", split_axis=1, concat_axis=1, tiled=True),
    )
    filled = arrived_marks.astype(jnp.float32).reshape(own_regions, REGION_SLOTS)

    def region_path(received):
        hidden = project_rows(received.reshape(slots_all, received.shape[-1]))
        hidden = hidden.reshape(own_regions, REGION_SLOTS, hidden.shape[-1])
        return region_layers(hidden, filled, w_qkv, w_attn_out, w_up, w_down, HEADS_R)

    pooled, region_back = jax.vjp(region_path, arrived)

    def front_rows(pooled_rows):
        return slide_front(pooled_rows, w_slide_in, w_slide_qkv)

    first_row = position * own_regions
    (token_rows, queries, key_values), front_back = jax.vjp(front_rows, pooled)
    all_keys = lax.all_gather(key_values, "tiles", axis=0, tiled=True)
    query_index = first_row + jnp.arange(own_regions, dtype=jnp.int32)
    query_slide = lax.dynamic_slice_in_dim(slide_of_region, first_row, own_regions)

    def mix_rows(token_part, query_part, key_part):
        return slide_mix(
            token_part,
            query_part,
            key_part,
            query_index,
            query_slide,
            slide_of_region,
            seg_offset,
            w_slide_out,
            HEADS_S,
        )

    slide_out, mix_back = jax.vjp(mix_rows, token_rows, queries, all_keys.astype(jnp.float32))
    grad_tokens, grad_queries, grad_keys = mix_back(slide_ct)
    own_key_grad = lax.psum_scatter(grad_keys, "tiles", scatter_dimension=0, tiled=True).astype(
        jnp.bfloat16
    )
    grad_pooled = front_back((grad_tokens, grad_queries, own_key_grad))[0]
    grad_arrived = region_back(grad_pooled)[0]
    returned = lax.all_to_all(grad_arrived, "tiles", split_axis=1, concat_axis=1, tiled=True)
    tile_grad = returned.reshape(slots_all, returned.shape[-1])[target]
    return (slide_out, tile_grad)


def solution(mesh):
    placed = (
        P(("groups", "tiles"), None),
        P(("groups", "tiles"), None),
        P("groups"),
        P(),
        P(),
        P(),
        P(),
        P(),
        P(),
        P(),
        P(),
        P(),
        P(("groups", "tiles"), None),
    )
    return jax.shard_map(
        local,
        mesh=mesh,
        in_specs=placed,
        out_specs=(P(("groups", "tiles"), None), P(("groups", "tiles"), None)),
        check_vma=False,
    )
```

profile of v0, /device:TPU:0, one launch (start us, length us, event | category | flops | bytes accessed | tf_op | source)
XLA Modules:
  0.0 245.9 jit_solution(17214906264226603378)
XLA Ops:
  0.7 1.5 fusion.98
  2.2 1.6 reduce_window_sum.11
  7.5 7.4 %all-to-all-start.1 = ((bf16[1,16,16]{2,0,1:T(2,128)(2,1)}), bf16[1,16,16]{2,0,1:T(2,128)(2,1)S(1)}, u32[]{:S(2)}, u32[]{:S(2)}) async-start(bf16[1,16,16]{2,0,1:T(2,128)(2,1)} %reshape.757), calls=%async_computation.1 | async-start | bytes 16384 | tf_op jit(solution)/shard_map/all_to_all | solution.py:145
  14.9 2.6 %scatter_custom_fusion = bf16[256,1536]{1,0:T(8,128)(2,1)} fusion(s32[128]{0:T(128)S(1)} %fusion.145, bf16[128,1536]{1,0:T(8,128)(2,1)} %param.13, bf16[]{:T(256)} %constant.106.clone.1), kind=kCustom, calls=%fused_computation.105 | custom fusion | bytes 786944 | tf_op jit(solution)/shard_map/scatter | solution.py:135
  17.5 3.7 %all-to-all-done.1 = bf16[1,16,16]{2,0,1:T(2,128)(2,1)S(1)} async-done(((bf16[1,16,16]{2,0,1:T(2,128)(2,1)}), bf16[1,16,16]{2,0,1:T(2,128)(2,1)S(1)}, u32[]{:S(2)}, u32[]{:S(2)}) %all-to-all-start.1) | async-done | bytes 544 | tf_op jit(solution)/shard_map/all_to_all | solution.py:145
  21.2 4.3 %all-to-all-start = ((bf16[1,16,16,1536]{3,2,0,1:T(8,128)(2,1)}), bf16[1,16,16,1536]{3,2,0,1:T(8,128)(2,1)}, u32[]{:S(2)}, u32[]{:S(2)}) async-start(bf16[1,16,16,1536]{3,2,0,1:T(8,128)(2,1)} %bitcast.200), calls=%async_computation | async-start | bytes 1572864 | tf_op jit(solution)/shard_map/all_to_all | solution.py:138
  25.6 1.7 convolution_reduce_fusion.3
  31.1 1.9 iota_compare_fusion.1
  33.8 10.4 %all-to-all-done = bf16[1,16,16,1536]{3,2,0,1:T(8,128)(2,1)} async-done(((bf16[1,16,16,1536]{3,2,0,1:T(8,128)(2,1)}), bf16[1,16,16,1536]{3,2,0,1:T(8,128)(2,1)}, u32[]{:S(2)}, u32[]{:S(2)}) %all-to-all-start) | async-done | bytes 786464 | tf_op jit(solution)/shard_map/all_to_all | solution.py:138
  44.3 2.2 fusion.175
  49.2 2.1 copy.48
  53.0 1.9 convert_reduce_fusion
  54.9 1.5 convolution_convert_fusion.6
  67.4 21.4 %all-gather = bf16[16,1,1536]{2,1,0:T(2,128)(2,1)S(1)} all-gather(bf16[1,1,1536]{2,1,0:T(2,128)(2,1)S(1)} %slice_bitcast_fusion.9), channel_id=1, replica_groups=mesh['groups'=2,'tiles'=16] {'tiles'}, dimensions={0}, use_global_device_ids=true | all-gather | bytes 52224 | tf_op jit(solution)/shard_map/all_gather | solution.py:161
  89.5 1.5 reshape.694
  91.7 1.6 fusion.105
  101.6 1.5 reshape.692
  106.0 2.2 convolution_reduce_fusion.4
  108.2 1.6 fusion.99
  116.6 1.6 reshape.701
  119.6 1.6 reshape.699
  121.2 1.5 pad_add_fusion
  122.7 60.0 %all-reduce.7 = bf16[16,1536]{1,0:T(8,128)(2,1)} all-reduce(f32[16,1536]{1,0:T(8,128)} %pad_add_fusion), channel_id=2, replica_groups=mesh['groups'=2,'tiles'=16] {'tiles'}, use_global_device_ids=true, to_apply=%region_21.22.clone | all-reduce | flops 24576 | bytes 147456
  186.5 1.8 convolution_reduce_fusion.2
  197.2 5.2 %multiply_reduce_fusion.1 = (f32[256]{0:T(256)}, f32[256,384]{1,0:T(8,128)}) fusion(f32[256,384]{1,0:T(8,128)} %copy-done.7, f32[256]{0:T(256)} %copy-done.32, bf16[384,1536]{1,0:T(8,128)(2,1)} %param.20, f32[256,1536]{1,0:T(8,128)} %copy-done.14, bf16[1536,384]{1,0:T(8,128)(2,1)} %param.21, f32[384]{0:T(512)S(1)} %add_divide_fusion, f32[256]{0:T(256)} %copy-done.37), kind=kOutput, calls=%fused_computation.100 | convolution fusion | flops 612826880 | bytes 4723200 | tf_op jit(solution)/shard_map/transpose(jvp())/dot_general | solution.py:47
  205.2 2.0 convolution_convert_fusion.5
  207.2 1.7 copy.51
  208.9 1.7 convolution_bitcast_fusion
  218.1 1.6 convolution_convert_fusion
  219.6 4.3 %all-to-all-start.2 = ((bf16[1,16,16,1536]{3,2,0,1:T(8,128)(2,1)}), bf16[1,16,16,1536]{3,2,0,1:T(8,128)(2,1)}, u32[]{:S(2)}, u32[]{:S(2)}) async-start(bf16[1,16,16,1536]{3,2,0,1:T(8,128)(2,1)} %bitcast.201), calls=%async_computation.2 | async-start | bytes 1572864 | tf_op jit(solution)/shard_map/all_to_all | solution.py:185
  224.5 18.1 %all-to-all-done.2 = bf16[1,16,16,1536]{3,2,0,1:T(8,128)(2,1)} async-done(((bf16[1,16,16,1536]{3,2,0,1:T(8,128)(2,1)}), bf16[1,16,16,1536]{3,2,0,1:T(8,128)(2,1)}, u32[]{:S(2)}, u32[]{:S(2)}) %all-to-all-start.2) | async-done | bytes 786464 | tf_op jit(solution)/shard_map/all_to_all | solution.py:185
  242.6 3.2 %gather_fusion = bf16[128,1536]{1,0:T(8,128)(2,1)} fusion(bf16[256,1536]{1,0:T(8,128)(2,1)} %bitcast.60, s32[1024]{0:T(1024)S(1)} %pad_clamp_fusion), kind=kCustom, calls=%fused_computation | custom fusion | bytes 786944 | tf_op jit(solution)/shard_map/gather | solution.py:186
  (200 shorter events, 62.4 us)
Async XLA Ops:
  0.6 66.1 %copy-start = (bf16[768,2304]{1,0:T(8,128)(2,1)S(1)}, bf16[768,2304]{1,0:T(8,128)(2,1)}, u32[]{:S(2)}) copy-start(bf16[768,2304]{1,0:T(8,128)(2,1)} %param.23) | copy-start | bytes 10616836
  0.6 24.9 %copy-start.36 = (bf16[1,768]{1,0:T(2,128)(2,1)S(1)}, bf16[1,768]{1,0:T(2,128)(2,1)}, u32[]{:S(2)}) copy-start(bf16[1,768]{1,0:T(2,128)(2,1)} %param.25) | copy-start | bytes 4612
  5.5 20.1 %copy-start.51 = (s32[128]{0:T(128)}, s32[128]{0:T(128)S(1)}, u32[]{:S(2)}) copy-start(s32[128]{0:T(128)S(1)} %fusion.145) | copy-start | bytes 1540
  7.5 13.7 %all-to-all-start.1 = ((bf16[1,16,16]{2,0,1:T(2,128)(2,1)}), bf16[1,16,16]{2,0,1:T(2,128)(2,1)S(1)}, u32[]{:S(2)}, u32[]{:S(2)}) async-start(bf16[1,16,16]{2,0,1:T(2,128)(2,1)} %reshape.757), calls=%async_computation.1 | async-start | bytes 16384 | tf_op jit(solution)/shard_map/all_to_all | solution.py:145
  21.2 23.0 %all-to-all-start = ((bf16[1,16,16,1536]{3,2,0,1:T(8,128)(2,1)}), bf16[1,16,16,1536]{3,2,0,1:T(8,128)(2,1)}, u32[]{:S(2)}, u32[]{:S(2)}) async-start(bf16[1,16,16,1536]{3,2,0,1:T(8,128)(2,1)} %bitcast.200), calls=%async_computation | async-start | bytes 1572864 | tf_op jit(solution)/shard_map/all_to_all | solution.py:138
  33.8 24.0 %copy-start.37 = (f32[256]{0:T(256)}, f32[256]{0:T(256)S(1)}, u32[]{:S(2)}) copy-start(f32[256]{0:T(256)S(1)} %reshape.687) | copy-start | bytes 3076
  33.8 17.5 %copy-start.49 = (pred[256]{0:T(512)(128)(4,1)}, pred[256]{0:T(512)(128)(4,1)S(1)}, u32[]{:S(2)}) copy-start(pred[256]{0:T(512)(128)(4,1)S(1)} %broadcast_compare_fusion.2) | copy-start | bytes 772
  44.2 3.6 %copy-start.9 = (bf16[384,1152]{1,0:T(8,128)(2,1)S(1)}, bf16[384,1152]{1,0:T(8,128)(2,1)}, u32[]{:S(2)}) copy-start(bf16[384,1152]{1,0:T(8,128)(2,1)} %param.18) | copy-start | bytes 2654212
  52.7 2.2 copy-start.1
  53.0 3.4 %copy-start.20 = (f32[6,256]{1,0:T(8,128)}, f32[6,256]{1,0:T(8,128)S(1)}, u32[]{:S(2)}) copy-start(f32[6,256]{1,0:T(8,128)S(1)} %fusion.46) | copy-start | bytes 18436
  53.0 3.4 %copy-start.4 = (f32[256,384]{1,0:T(8,128)S(1)}, f32[256,384]{1,0:T(8,128)}, u32[]{:S(2)}) copy-start(f32[256,384]{1,0:T(8,128)} %copy-done.3) | copy-start | bytes 1179652
  53.0 3.4 %copy-start.15 = (bf16[384,384]{1,0:T(8,128)(2,1)S(1)}, bf16[384,384]{1,0:T(8,128)(2,1)}, u32[]{:S(2)}) copy-start(bf16[384,384]{1,0:T(8,128)(2,1)} %param.19) | copy-start | bytes 884740
  54.9 2.9 %copy-start.6 = (bf16[1,6,256,256]{2,3,1,0:T(8,128)(2,1)}, bf16[1,6,256,256]{2,3,1,0:T(8,128)(2,1)S(1)}, u32[]{:S(2)}) copy-start(bf16[1,6,256,256]{2,3,1,0:T(8,128)(2,1)S(1)} %get-tuple-element.18) | copy-start | bytes 2359300
  54.9 2.2 copy-start.16
  60.8 2.0 copy-start.23
  64.1 3.2 %copy-start.18 = (f32[768]{0:T(1024)}, f32[768]{0:T(1024)S(1)}, u32[]{:S(2)}) copy-start(f32[768]{0:T(1024)S(1)} %convolution_reduce_fusion.1) | copy-start | bytes 9220
  67.4 27.2 %copy-start.31 = (bf16[768]{0:T(1024)(128)(2,1)}, bf16[768]{0:T(1024)(128)(2,1)S(1)}, u32[]{:S(2)}) copy-start(bf16[768]{0:T(1024)(128)(2,1)S(1)} %slice_reduce_fusion) | copy-start | bytes 4612
  186.5 1.8 copy-start.19
  186.5 3.0 %copy-start.34 = (f32[768]{0:T(1024)S(1)}, f32[768]{0:T(1024)}, u32[]{:S(2)}) copy-start(f32[768]{0:T(1024)} %convolution_reduce_fusion.4) | copy-start | bytes 9220
  186.5 6.8 %copy-start.24 = (f32[384]{0:T(512)S(1)}, f32[384]{0:T(512)}, u32[]{:S(2)}) copy-start(f32[384]{0:T(512)} %copy-done.23) | copy-start | bytes 4612
  193.3 2.5 copy-start.35
  197.2 7.3 %copy-start.28 = (f32[384]{0:T(512)}, f32[384]{0:T(512)S(1)}, u32[]{:S(2)}) copy-start(f32[384]{0:T(512)S(1)} %add_divide_fusion) | copy-start | bytes 4612
  197.2 5.9 %copy-start.33 = (f32[256]{0:T(256)S(1)}, f32[256]{0:T(256)}, u32[]{:S(2)}) copy-start(f32[256]{0:T(256)} %copy-done.32) | copy-start | bytes 3076
  207.2 4.9 %copy-start.21 = (f32[6,256]{1,0:T(8,128)S(1)}, f32[6,256]{1,0:T(8,128)}, u32[]{:S(2)}) copy-start(f32[6,256]{1,0:T(8,128)} %copy-done.20) | copy-start | bytes 18436
  208.9 3.2 %copy-start.2 = (f32[6,256,256]{1,2,0:T(8,128)S(1)}, f32[6,256,256]{1,2,0:T(8,128)}, u32[]{:S(2)}) copy-start(f32[6,256,256]{1,2,0:T(8,128)} %copy-done.1) | copy-start | bytes 4718596
  215.5 1.8 copy-start.45
  215.5 1.8 copy-start.42
  216.7 1.3 copy-start.12
  216.7 1.3 copy-start.29
  218.0 5.9 %copy-start.52 = (s32[128]{0:T(128)S(1)}, s32[128]{0:T(128)}, u32[]{:S(2)}) copy-start(s32[128]{0:T(128)} %copy-done.51) | copy-start | bytes 1540
  218.1 5.9 %copy-start.48 = (bf16[768]{0:T(1024)(128)(2,1)S(1)}, bf16[768]{0:T(1024)(128)(2,1)}, u32[]{:S(2)}) copy-start(bf16[768]{0:T(1024)(128)(2,1)} %get-tuple-element.22) | copy-start | bytes 4612
  219.6 23.0 %all-to-all-start.2 = ((bf16[1,16,16,1536]{3,2,0,1:T(8,128)(2,1)}), bf16[1,16,16,1536]{3,2,0,1:T(8,128)(2,1)}, u32[]{:S(2)}, u32[]{:S(2)}) async-start(bf16[1,16,16,1536]{3,2,0,1:T(8,128)(2,1)} %bitcast.201), calls=%async_computation.2 | async-start | bytes 1572864 | tf_op jit(solution)/shard_map/all_to_all | solution.py:185
  (25 other events, 23.6 us)
where the time goes:
time: 248 us; the launch traced here: 246 us
  blocking collectives  81.4 us (33%)
  local copies, waits for them, and re-layouts  41 us (17%)
  matrix products  36.5 us (15%)
  other arithmetic  32.2 us (13%)
  waiting for transfers between devices  32.2 us (13%)
  starting transfers between devices  16 us (6%)
  between operations  6.66 us (3%)
    unnamed x1, blocking collectives  60 us
    all_gather x1, blocking collectives, local(): all_keys = lax.all_gather(key_values, 'tiles', axis=0, tiled=True)  21.4 us
    all_to_all x1, waiting for transfers between devices, local(): lax.all_to_all(grad_arrived, 'tiles', split_axis=1, concat_axis=1, tiled=...  18.1 us
    all_to_all x1, waiting for transfers between devices, local(): lax.all_to_all(outgoing.reshape(layout + (tiles.shape[1],)), 'tiles', spl...  10.4 us
    unnamed x111, local copies, waits for them, and re-layouts  7.62 us
    all_to_all x1, starting transfers between devices, local(): lax.all_to_all(marks.reshape(layout), 'tiles', split_axis=1, concat_axis=...  7.39 us
    another operation x7, local copies, waits for them, and re-layouts  6.27 us
    dot_general x2, matrix products, region_layers(): jnp.dot(normed_two, w_up, preferred_element_type=jnp.float32)  5.82 us
  transfers between devices with their start and end apart: 3, of which 3 were waited for; matrix products, arithmetic and copies ran while one was open for 5% of the time, Pallas kernels for 0%

commit v1 on v0

v1 whole, which is shorter than its diff:
```python
import functools

import jax
import jax.numpy as jnp
from jax import lax
from jax.experimental import pallas as pl
from jax.experimental.pallas import tpu as pltpu
from jax.sharding import PartitionSpec as P

HEADS_R = 6
HEADS_S = 12
REGION_SLOTS = 256
DILATION = 4
EMPTY = 1e30
F32 = jnp.float32
BF16 = jnp.bfloat16
MESH = pl.DeviceIdType.MESH


def mm(a, b):
    return jnp.dot(a, b, preferred_element_type=F32)


def mm_nt(a, b):
    return lax.dot_general(a, b, (((1,), (1,)), ((), ())), preferred_element_type=F32)


def mm_tn(a, b):
    return lax.dot_general(a, b, (((0,), (0,)), ((), ())), preferred_element_type=F32)


def norm(x):
    mean = jnp.mean(x, axis=-1, keepdims=True)
    centred = x - mean
    scale = lax.rsqrt(jnp.mean(centred * centred, axis=-1, keepdims=True) + 1e-05)
    return centred * scale, scale


def norm_back(grad, normed, scale):
    grad = grad.astype(BF16).astype(F32)
    return scale * (
        grad
        - jnp.mean(grad, axis=-1, keepdims=True)
        - normed * jnp.mean(grad * normed, axis=-1, keepdims=True)
    )


def softmax(scores):
    raised = jnp.exp(scores - jnp.max(scores, axis=-1, keepdims=True))
    return raised / jnp.sum(raised, axis=-1, keepdims=True)


def softmax_back(weights, grad):
    grad = grad.astype(BF16).astype(F32)
    return weights * (grad - jnp.sum(grad * weights, axis=-1, keepdims=True))


def iota(shape, axis):
    return lax.broadcasted_iota(jnp.int32, shape, axis)


def kernel(
    n,
    chunk,
    tiles_ref,
    region_ref,
    slides_ref,
    offset_ref,
    ct_ref,
    w_in_hbm,
    w_qkv_hbm,
    w_attn_out_hbm,
    w_up_hbm,
    w_down_hbm,
    w_slide_in_hbm,
    w_slide_qkv_hbm,
    w_slide_out_hbm,
    slide_out_ref,
    grad_ref,
    w_in,
    w_qkv,
    w_attn_out,
    w_up,
    w_down,
    w_slide_in,
    w_slide_qkv,
    w_slide_out,
    send_x,
    recv_x,
    send_g,
    recv_g,
    ct_all,
    pool_own,
    pool_all,
    up_out,
    up_slope,
    w_sem,
    x_send_sem,
    x_recv_sem,
    g_send_sem,
    g_recv_sem,
    c_send_sem,
    c_recv_sem,
    p_send_sem,
    p_recv_sem,
):
    me = lax.axis_index("tiles")
    barrier = pltpu.get_barrier_semaphore()

    def at(peer):
        return {"tiles": peer}

    def greet(step, carry):
        pl.semaphore_signal(
            barrier, inc=1, device_id=at(lax.rem(me + step, n)), device_id_type=MESH
        )
        return carry

    lax.fori_loop(1, n, greet, 0)

    loads = [
        pltpu.make_async_copy(source, target, w_sem.at[i])
        for i, (source, target) in enumerate(
            [
                (w_in_hbm, w_in),
                (w_qkv_hbm, w_qkv),
                (w_attn_out_hbm, w_attn_out),
                (w_up_hbm, w_up),
                (w_down_hbm, w_down),
                (w_slide_in_hbm, w_slide_in),
                (w_slide_qkv_hbm, w_slide_qkv),
                (w_slide_out_hbm, w_slide_out),
            ]
        )
    ]
    for load in loads:
        load.start()

    rows, width = tiles_ref.shape[0], w_in.shape[1]
    slots_sent = n * chunk
    capacity = REGION_SLOTS // n

    region = region_ref[...]
    named = (iota((n, rows), 0) == region).astype(F32)
    earlier = (iota((rows, rows), 0) < iota((rows, rows), 1)).astype(BF16)
    before = mm(named.astype(BF16), earlier)
    rank = jnp.sum(before * named, axis=0, keepdims=True)
    target = region.astype(F32) * chunk + rank
    place = iota((slots_sent, rows), 0).astype(F32) == target
    held = jnp.max(place.astype(F32), axis=1, keepdims=True) > 0
    place = place.astype(BF16)

    def everyone(body):
        def step_body(step, carry):
            body(lax.rem(me + step, n))
            return carry

        lax.fori_loop(1, n, step_body, 0)

    def exchange(source, target_all, send_sem, recv_sem, peer):
        return pltpu.make_async_remote_copy(
            src_ref=source,
            dst_ref=target_all.at[me],
            send_sem=send_sem.at[peer],
            recv_sem=recv_sem.at[me],
            device_id=at(peer),
            device_id_type=MESH,
        )

    def arrival(source, target_all, send_sem, recv_sem, peer):
        return pltpu.make_async_remote_copy(
            src_ref=source,
            dst_ref=target_all.at[peer],
            send_sem=send_sem.at[peer],
            recv_sem=recv_sem.at[peer],
            device_id=at(peer),
            device_id_type=MESH,
        )

    loads[0].wait()
    projected = mm(tiles_ref[...], w_in[...]).astype(BF16)
    outgoing = jnp.where(held, mm(place, projected), EMPTY).astype(BF16)
    send_x[...] = outgoing.reshape(n, chunk, width)

    pl.semaphore_wait(barrier, n - 1)

    def start_x(peer):
        exchange(send_x.at[peer], recv_x, x_send_sem, x_recv_sem, peer).start()

    everyone(start_x)

    def start_ct(peer):
        exchange(ct_ref, ct_all, c_send_sem, c_recv_sem, peer).start()

    everyone(start_ct)
    recv_x[me] = send_x[me]
    ct_all[me] = ct_ref[...]
    square = iota((rows, rows), 0) == iota((rows, rows), 1)
    target_col = jnp.sum(jnp.where(square, target, 0.0), axis=1, keepdims=True)
    fetch = (iota((rows, slots_sent), 1).astype(F32) == target_col).astype(BF16)
    if chunk != capacity:
        slot = iota((REGION_SLOTS, slots_sent), 0)
        pick = (
            iota((REGION_SLOTS, slots_sent), 1) == slot // capacity * chunk + slot % capacity
        ).astype(BF16)

    for load in loads[1:5]:
        load.wait()

    def wait_x(peer):
        arrival(send_x.at[peer], recv_x, x_send_sem, x_recv_sem, peer).wait_recv()

    everyone(wait_x)

    arrived = recv_x[...].reshape(slots_sent, width)
    if chunk != capacity:
        arrived = mm(pick, arrived)
    else:
        arrived = arrived.astype(F32)
    filled = arrived[:, :1] < 0.5 * EMPTY
    filled_col = filled.astype(F32)
    hidden = jnp.where(filled, arrived, 0.0)
    filled_lanes = jnp.broadcast_to(filled_col, (REGION_SLOTS, 128)).astype(BF16)
    filled_row = mm_nt(jnp.ones((16, 128), BF16), filled_lanes)[:1] > 0
    counted = jnp.sum(filled_col, axis=0, keepdims=True)

    normed, scale = norm(hidden)
    packed = mm(normed.astype(BF16), w_qkv[...]).astype(BF16)
    head_size = width // HEADS_R
    factor = head_size**-0.5
    lane = iota((REGION_SLOTS, 128), 1) // head_size
    per = 128 // head_size
    nothing = jnp.zeros((REGION_SLOTS, 128), BF16)
    weights, mixed = [], []
    for pair in range(HEADS_R // per):
        columns = [slice(part * width + pair * 128, part * width + pair * 128 + 128) for part in range(3)]
        q, k, v = (packed[:, c] for c in columns)
        total = None
        for h in range(per):
            scores = mm_nt(jnp.where(lane == h, q, nothing), k) * factor
            chances = softmax(jnp.where(filled_row, scores, -1e30))
            weights.append(chances)
            term = mm(chances.astype(BF16), jnp.where(lane == h, v, nothing))
            total = term if total is None else total + term
        mixed.append(total.astype(BF16))
    mixed = jnp.concatenate(mixed, axis=1)
    first = hidden + mm(mixed, w_attn_out[...])
    normed_two, scale_two = norm(first)
    rounded_two = normed_two.astype(BF16)
    hidden_units = w_up.shape[1]
    block = width
    gate = 0.7978845608028654
    second_sum = jnp.sum(first * filled_col, axis=0, keepdims=True)
    inner_sums = []
    for c in range(0, hidden_units, block):
        u = mm(rounded_two, w_up[:, c : c + block])
        up_out[:, c : c + block] = u
        bent = jnp.tanh(gate * (u + 0.044715 * u * u * u))
        inner = (0.5 * u * (1.0 + bent)).astype(BF16).astype(F32)
        inner_sums.append(jnp.sum(inner * filled_col, axis=0, keepdims=True))
        up_slope[:, c : c + block] = bent
    inner_sum = jnp.concatenate(inner_sums, axis=1)
    high = inner_sum.astype(BF16)
    low = (inner_sum - high.astype(F32)).astype(BF16)
    both = jnp.concatenate([jnp.broadcast_to(high, (16, hidden_units)), jnp.broadcast_to(low, (16, hidden_units))], axis=0)
    down = mm(both, w_down[...])
    pooled = (second_sum + down[:1] + down[16:17]) / counted
    pool_own[...] = jnp.zeros_like(pool_own)
    for i in range(width // 128):
        pool_own[i : i + 1, :] = pooled[:, i * 128 : i * 128 + 128]

    def start_pool(peer):
        exchange(pool_own, pool_all, p_send_sem, p_recv_sem, peer).start()

    everyone(start_pool)
    pool_all[me] = pool_own[...]

    for c in range(0, hidden_units, block):
        u = up_out[:, c : c + block]
        bent = up_slope[:, c : c + block]
        slope = 0.5 * (1.0 + bent) + 0.5 * u * (1.0 - bent * bent) * gate * (
            1.0 + 3 * 0.044715 * u * u
        )
        up_slope[:, c : c + block] = slope * filled_col

    for load in loads[5:]:
        load.wait()

    def wait_pool(peer):
        arrival(ct_ref, ct_all, c_send_sem, c_recv_sem, peer).wait_recv()
        arrival(pool_own, pool_all, p_send_sem, p_recv_sem, peer).wait_recv()

    everyone(wait_pool)

    slide_width = w_slide_in.shape[1]
    pooled_rows = jnp.concatenate([pool_all[:, i, :] for i in range(width // 128)], axis=1)
    ct = jnp.concatenate([ct_all[:, i, :] for i in range(slide_width // 128)], axis=1)
    pool_normed, pool_scale = norm(pooled_rows)
    token = mm(pool_normed.astype(BF16), w_slide_in[...])
    token_normed, token_scale = norm(token)
    slide_packed = mm(token_normed.astype(BF16), w_slide_qkv[...]).astype(BF16)
    sq = slide_packed[:, :slide_width].astype(F32)
    sk = slide_packed[:, slide_width : 2 * slide_width]
    sv = slide_packed[:, 2 * slide_width :]
    slide_size = slide_width // HEADS_S
    slide_factor = slide_size**-0.5
    slide_lane = iota((n, slide_width), 1) // slide_size

    def spread(values):
        return jnp.concatenate(
            [jnp.where(slide_lane == h, values, 0.0) for h in range(HEADS_S)], axis=0
        ).astype(BF16)

    def gather(values):
        total = None
        for h in range(HEADS_S):
            term = jnp.where(slide_lane == h, values[h * n : h * n + n], 0.0)
            total = term if total is None else total + term
        return total

    slides_row = slides_ref[...]
    own = iota((n, n), 0) == iota((n, n), 1)
    slides_col = jnp.sum(jnp.where(own, slides_row, 0), axis=1, keepdims=True)
    same = slides_col == slides_row
    key_index = iota((n, n), 1)
    allowed = jnp.concatenate(
        [
            jnp.where(
                same & ((lax.rem(key_index + offset_ref[h], DILATION) == 0) | own), 1.0, 0.0
            )
            for h in range(HEADS_S)
        ],
        axis=0,
    )
    sq_heads = spread(sq)
    slide_scores = mm_nt(sq_heads, sk) * slide_factor
    slide_weights = softmax(jnp.where(allowed > 0, slide_scores, -1e30))
    slide_rounded = slide_weights.astype(BF16)
    slide_mixed = gather(mm(slide_rounded, sv)).astype(BF16)
    slide_out = token + mm(slide_mixed, w_slide_out[...])
    mine = iota((n, 1), 0) == me
    slide_out_ref[...] = jnp.sum(
        jnp.where(mine, slide_out, 0.0), axis=0, keepdims=True
    ).astype(BF16)

    g_mixed = mm_nt(ct.astype(BF16), w_slide_out[...]).astype(BF16).astype(F32)
    g_heads = spread(g_mixed)
    g_scores = softmax_back(slide_weights, mm_nt(g_heads, sv)) * slide_factor
    g_scores = g_scores.astype(BF16)
    g_q = gather(mm(g_scores, sk))
    g_k = mm_tn(g_scores, sq_heads)
    g_v = mm_tn(slide_rounded, g_heads)
    g_packed = jnp.concatenate([g_q, g_k, g_v], axis=1).astype(BF16)
    g_token = ct + norm_back(mm_nt(g_packed, w_slide_qkv[...]), token_normed, token_scale)
    g_pooled = norm_back(
        mm_nt(g_token.astype(BF16), w_slide_in[...]), pool_normed, pool_scale
    )
    g_pooled = jnp.sum(jnp.where(mine, g_pooled, 0.0), axis=0, keepdims=True) / counted

    g_inner = mm_nt(jnp.broadcast_to(g_pooled, (16, width)).astype(BF16), w_down[...])[:1]
    g_inner = g_inner.astype(BF16).astype(F32)
    g_two = None
    for c in range(0, hidden_units, block):
        g_up = (up_slope[:, c : c + block] * g_inner[:, c : c + block]).astype(BF16)
        term = mm_nt(g_up, w_up[:, c : c + block])
        g_two = term if g_two is None else g_two + term
    g_first = g_pooled * filled_col + norm_back(g_two, normed_two, scale_two)
    g_mixed = mm_nt(g_first.astype(BF16), w_attn_out[...]).astype(BF16)
    g_qs, g_ks, g_vs = [], [], []
    for pair in range(HEADS_R // per):
        columns = [slice(part * width + pair * 128, part * width + pair * 128 + 128) for part in range(3)]
        q, k, v = (packed[:, c] for c in columns)
        g_pair = g_mixed[:, pair * 128 : pair * 128 + 128]
        sums = None
        for h in range(per):
            chances = weights[pair * per + h]
            g_h = jnp.where(lane == h, g_pair, nothing)
            q_h = jnp.where(lane == h, q, nothing)
            k_h = jnp.where(lane == h, k, nothing)
            g_s = (softmax_back(chances, mm_nt(g_h, v)) * factor).astype(BF16)
            terms = (mm(g_s, k_h), mm_tn(g_s, q_h), mm_tn(chances.astype(BF16), g_h))
            sums = terms if sums is None else tuple(a + b for a, b in zip(sums, terms))
        g_qs.append(sums[0])
        g_ks.append(sums[1])
        g_vs.append(sums[2])
    g_packed = jnp.concatenate(g_qs + g_ks + g_vs, axis=1).astype(BF16)
    g_hidden = g_first + norm_back(mm_nt(g_packed, w_qkv[...]), normed, scale)
    g_hidden = g_hidden.astype(BF16)
    if chunk != capacity:
        g_hidden = mm_tn(pick, g_hidden).astype(BF16)
    send_g[...] = g_hidden.reshape(n, chunk, width)

    def start_g(peer):
        exchange(send_g.at[peer], recv_g, g_send_sem, g_recv_sem, peer).start()

    everyone(start_g)
    recv_g[me] = send_g[me]

    def wait_sent(peer):
        exchange(send_x.at[peer], recv_x, x_send_sem, x_recv_sem, peer).wait_send()
        exchange(ct_ref, ct_all, c_send_sem, c_recv_sem, peer).wait_send()
        exchange(pool_own, pool_all, p_send_sem, p_recv_sem, peer).wait_send()

    everyone(wait_sent)

    def wait_g(peer):
        arrival(send_g.at[peer], recv_g, g_send_sem, g_recv_sem, peer).wait_recv()

    everyone(wait_g)
    returned = mm(fetch, recv_g[...].reshape(slots_sent, width)).astype(BF16)
    grad_ref[...] = mm_nt(returned, w_in[...]).astype(BF16)

    def wait_g_sent(peer):
        exchange(send_g.at[peer], recv_g, g_send_sem, g_recv_sem, peer).wait_send()

    everyone(wait_g_sent)


def local(
    tiles,
    tile_region,
    slide_of_region,
    seg_offset,
    w_in,
    w_qkv,
    w_attn_out,
    w_up,
    w_down,
    w_slide_in,
    w_slide_qkv,
    w_slide_out,
    slide_ct,
):
    n = lax.axis_size("tiles")
    rows, depth = tiles.shape
    width, hidden_units, slide_width = w_in.shape[1], w_up.shape[1], w_slide_in.shape[1]
    assert slide_ct.shape[0] == 1 and slide_of_region.shape[0] == n
    chunk = max(16, REGION_SLOTS // n)
    ct = jnp.pad(
        slide_ct.astype(F32).reshape(slide_width // 128, 128), ((0, 8 - slide_width // 128), (0, 0))
    )
    weights = (w_in, w_qkv, w_attn_out, w_up, w_down, w_slide_in, w_slide_qkv, w_slide_out)
    vmem = pl.BlockSpec(memory_space=pltpu.VMEM)
    dma = pltpu.SemaphoreType.DMA
    return pl.pallas_call(
        functools.partial(kernel, n, chunk),
        out_shape=(
            jax.ShapeDtypeStruct((1, slide_width), BF16),
            jax.ShapeDtypeStruct((rows, depth), BF16),
        ),
        in_specs=[vmem, vmem, vmem, pl.BlockSpec(memory_space=pltpu.SMEM), vmem]
        + [pl.BlockSpec(memory_space=pl.ANY)] * len(weights),
        out_specs=(vmem, vmem),
        scratch_shapes=[pltpu.VMEM(w.shape, BF16) for w in weights]
        + [pltpu.VMEM((n, chunk, width), BF16)] * 4
        + [
            pltpu.VMEM((n, 8, 128), F32),
            pltpu.VMEM((8, 128), F32),
            pltpu.VMEM((n, 8, 128), F32),
            pltpu.VMEM((REGION_SLOTS, hidden_units), F32),
            pltpu.VMEM((REGION_SLOTS, hidden_units), F32),
            dma((len(weights),)),
        ]
        + [dma((n,))] * 8,
        compiler_params=pltpu.CompilerParams(
            collective_id=0, has_side_effects=True, vmem_limit_bytes=56 * 1024 * 1024
        ),
        cost_estimate=pl.CostEstimate(
            flops=2_000_000_000, bytes_accessed=12_000_000, transcendentals=800_000
        ),
    )(
        tiles,
        tile_region.reshape(1, rows),
        slide_of_region.reshape(1, n),
        seg_offset,
        ct,
        *weights,
    )


def solution(mesh):
    placed = (
        P(("groups", "tiles"), None),
        P(("groups", "tiles"), None),
        P("groups"),
        P(),
        P(),
        P(),
        P(),
        P(),
        P(),
        P(),
        P(),
        P(),
        P(("groups", "tiles"), None),
    )
    return jax.shard_map(
        local,
        mesh=mesh,
        in_specs=placed,
        out_specs=(P(("groups", "tiles"), None), P(("groups", "tiles"), None)),
        check_vma=False,
    )
```

time: 248 us -> 42.2 us (0.17)
  blocking collectives: 81.4 us -> 0 us
  local copies, waits for them, and re-layouts: 41 us -> 3.01 us
  Pallas kernels: 0 us -> 37 us
  matrix products: 36.5 us -> 0 us
  waiting for transfers between devices: 32.2 us -> 0 us
  other arithmetic: 32.2 us -> 1.3 us
  starting transfers between devices: 16 us -> 0 us
  between operations: 6.66 us -> 0.64 us
    unnamed x1 -> x0, blocking collectives: 60 us -> none
    pallas_call x0 -> x1, Pallas kernels: none -> 37 us  [local(): pl.pallas_call(functools.partial(kernel, n, chunk), out_shape=(jax.ShapeD...]
    dot_general x25 -> x0, matrix products: 36.5 us -> none  [the longest x2 5.82 us: region_layers(): jnp.dot(normed_two, w_up, preferred_element_type=jnp.float32)]
    all_to_all x3 -> x0, waiting for transfers between devices: 32.2 us -> none  [the longest x1 18.1 us: local(): lax.all_to_all(grad_arrived, 'tiles', split_axis=1, concat_axis=1, tiled=...]
    all_gather x1 -> x0, blocking collectives: 21.4 us -> none  [local(): all_keys = lax.all_gather(key_values, 'tiles', axis=0, tiled=True)]
    all_to_all x3 -> x0, starting transfers between devices: 16 us -> none  [the longest x1 7.39 us: local(): lax.all_to_all(marks.reshape(layout), 'tiles', split_axis=1, concat_axis=...]
    reduce_sum x22 -> x0, other arithmetic: 15.3 us -> none  [the longest x4 3.46 us: layer_norm(): centred = values - average]
    reshape x6 -> x0, local copies, waits for them, and re-layouts: 6.91 us -> none  [the longest x2 3.08 us: slide_mix(): values_part = key_values[:, width:].reshape(count, head_count, head_size)]
  transfers between devices with their start and end apart: 3 -> 0, of which waited for: 3 -> 0; matrix products, arithmetic and copies ran while one was open for 5% -> 0% of each run, Pallas kernels for 0% -> 0%
where the time goes in v1:
time: 42.2 us; the launch traced here: 42 us
  Pallas kernels  37 us (88%)
  local copies, waits for them, and re-layouts  3.01 us (7%)
  other arithmetic  1.3 us (3%)
  between operations  0.64 us (2%)
    pallas_call x1, Pallas kernels, local(): pl.pallas_call(functools.partial(kernel, n, chunk), out_shape=(jax.ShapeD...  37 us
    unnamed x2, local copies, waits for them, and re-layouts  3.01 us

profile of v1, /device:TPU:0, one launch (start us, length us, event | category | flops | bytes accessed | tf_op | source)
XLA Modules:
  0.0 42.0 jit_solution(4880624139888918174)
XLA Ops:
  0.6 0.7 %reduce = bf16[768]{0:T(1024)(128)(2,1)S(1)} reduce(bf16[1,768]{1,0:T(2,128)(2,1)} %param.25, bf16[]{:T(256)} %constant.7), dimensions={0}, to_apply=%param.25.reduce_sub_computation | reduce | bytes 3074 | tf_op args[12]
  1.3 0.6 %pad_convert_fusion.ct_ref = f32[8,128]{1,0:T(8,128)} fusion(bf16[6,128]{1,0:T(8,128)(2,1)S(1)} %bitcast.3), kind=kLoop, calls=%fused_computation | loop fusion | flops 1024 | bytes 5632 | tf_op jit(solution)/shard_map/jit(_pad)/pad | solution.py:439
  1.9 37.0 %shard_map.140 = (bf16[1,768]{1,0:T(2,128)(2,1)}, bf16[128,1536]{1,0:T(8,128)(2,1)}) custom-call(bf16[128,1536]{1,0:T(8,128)(2,1)} %tiles_ref.1, s32[1,128]{1,0:T(1,128)} %bitcast.4, s32[1,16]{1,0:T(1,128)} %bitcast.5, s32[12]{0:T(128)} %offset_ref.1, f32[8,128]{1,0:T(8,128)} %pad_convert_fusion.ct_ref, bf16[1536,384]{1,0:T(8,128)(2,1)} %w_in_hbm.1, ...), custom_call_target="tpu_custom_call" | custom-call | flops 2000000000 | bytes 12000000 | tf_op jit(solution)/shard_map/pallas_call | solution.py:445
  39.0 1.2 %copy.17 = bf16[1,768]{1,0:T(2,128)(2,1)} copy(bf16[1,768]{1,0:T(2,128)(2,1)} %get-tuple-element.4) | data formatting | bytes 3072
  40.2 1.8 %copy.18 = bf16[128,1536]{1,0:T(8,128)(2,1)} copy(bf16[128,1536]{1,0:T(8,128)(2,1)} %get-tuple-element.5) | data formatting | bytes 786432

commit v2 on v1

--- a/solution.py
+++ b/solution.py
@@ -76,7 +76,7 @@
     w_slide_qkv_hbm,
     w_slide_out_hbm,
     slide_out_ref,
-    grad_ref,
+    returned_ref,
     w_in,
     w_qkv,
     w_attn_out,
@@ -89,7 +89,6 @@
     recv_x,
     send_g,
     recv_g,
-    ct_all,
     pool_own,
     pool_all,
     up_out,
@@ -99,8 +98,6 @@
     x_recv_sem,
     g_send_sem,
     g_recv_sem,
-    c_send_sem,
-    c_recv_sem,
     p_send_sem,
     p_recv_sem,
 ):
@@ -189,12 +186,8 @@
 
     everyone(start_x)
 
-    def start_ct(peer):
-        exchange(ct_ref, ct_all, c_send_sem, c_recv_sem, peer).start()
-
-    everyone(start_ct)
     recv_x[me] = send_x[me]
-    ct_all[me] = ct_ref[...]
+    pool_own[:, width:] = ct_ref[...].astype(F32)
     square = iota((rows, rows), 0) == iota((rows, rows), 1)
     target_col = jnp.sum(jnp.where(square, target, 0.0), axis=1, keepdims=True)
     fetch = (iota((rows, slots_sent), 1).astype(F32) == target_col).astype(BF16)
@@ -265,9 +258,7 @@
     both = jnp.concatenate([jnp.broadcast_to(high, (16, hidden_units)), jnp.broadcast_to(low, (16, hidden_units))], axis=0)
     down = mm(both, w_down[...])
     pooled = (second_sum + down[:1] + down[16:17]) / counted
-    pool_own[...] = jnp.zeros_like(pool_own)
-    for i in range(width // 128):
-        pool_own[i : i + 1, :] = pooled[:, i * 128 : i * 128 + 128]
+    pool_own[:, :width] = pooled
 
     def start_pool(peer):
         exchange(pool_own, pool_all, p_send_sem, p_recv_sem, peer).start()
@@ -287,14 +278,13 @@
         load.wait()
 
     def wait_pool(peer):
-        arrival(ct_ref, ct_all, c_send_sem, c_recv_sem, peer).wait_recv()
         arrival(pool_own, pool_all, p_send_sem, p_recv_sem, peer).wait_recv()
 
     everyone(wait_pool)
 
     slide_width = w_slide_in.shape[1]
-    pooled_rows = jnp.concatenate([pool_all[:, i, :] for i in range(width // 128)], axis=1)
-    ct = jnp.concatenate([ct_all[:, i, :] for i in range(slide_width // 128)], axis=1)
+    pooled_rows = pool_all[:, 0, :width]
+    ct = pool_all[:, 0, width:]
     pool_normed, pool_scale = norm(pooled_rows)
     token = mm(pool_normed.astype(BF16), w_slide_in[...])
     token_normed, token_scale = norm(token)
@@ -398,7 +388,6 @@
 
     def wait_sent(peer):
         exchange(send_x.at[peer], recv_x, x_send_sem, x_recv_sem, peer).wait_send()
-        exchange(ct_ref, ct_all, c_send_sem, c_recv_sem, peer).wait_send()
         exchange(pool_own, pool_all, p_send_sem, p_recv_sem, peer).wait_send()
 
     everyone(wait_sent)
@@ -407,13 +396,37 @@
         arrival(send_g.at[peer], recv_g, g_send_sem, g_recv_sem, peer).wait_recv()
 
     everyone(wait_g)
-    returned = mm(fetch, recv_g[...].reshape(slots_sent, width)).astype(BF16)
-    grad_ref[...] = mm_nt(returned, w_in[...]).astype(BF16)
+    returned_ref[...] = mm(fetch, recv_g[...].reshape(slots_sent, width)).astype(BF16)
 
     def wait_g_sent(peer):
         exchange(send_g.at[peer], recv_g, g_send_sem, g_recv_sem, peer).wait_send()
 
     everyone(wait_g_sent)
+
+
+def finish(
+    slide_hbm, returned_hbm, w_in_hbm, slide_out_ref, grad_hbm, returned, w_in, grad, sem, w_sem, out_sem
+):
+    blocks = range(grad.shape[0])
+    slide_copy = pltpu.make_async_copy(slide_hbm, slide_out_ref, sem.at[0])
+    returned_copy = pltpu.make_async_copy(returned_hbm, returned, sem.at[1])
+    loads = [pltpu.make_async_copy(w_in_hbm.at[i * 512 : i * 512 + 512], w_in.at[i], w_sem.at[i]) for i in blocks]
+    returned_copy.start()
+    for load in loads:
+        load.start()
+    slide_copy.start()
+    returned_copy.wait()
+    copies = []
+    for i in blocks:
+        loads[i].wait()
+        grad[i] = mm_nt(returned[...], w_in[i]).astype(BF16)
+        copies.append(
+            pltpu.make_async_copy(grad.at[i], grad_hbm.at[:, i * 512 : i * 512 + 512], out_sem.at[i])
+        )
+        copies[i].start()
+    slide_copy.wait()
+    for copy in copies:
+        copy.wait()
 
 
 def local(
@@ -436,32 +449,29 @@
     width, hidden_units, slide_width = w_in.shape[1], w_up.shape[1], w_slide_in.shape[1]
     assert slide_ct.shape[0] == 1 and slide_of_region.shape[0] == n
     chunk = max(16, REGION_SLOTS // n)
-    ct = jnp.pad(
-        slide_ct.astype(F32).reshape(slide_width // 128, 128), ((0, 8 - slide_width // 128), (0, 0))
-    )
     weights = (w_in, w_qkv, w_attn_out, w_up, w_down, w_slide_in, w_slide_qkv, w_slide_out)
     vmem = pl.BlockSpec(memory_space=pltpu.VMEM)
+    anywhere = pl.BlockSpec(memory_space=pl.ANY)
     dma = pltpu.SemaphoreType.DMA
-    return pl.pallas_call(
+    slide_row, returned = pl.pallas_call(
         functools.partial(kernel, n, chunk),
         out_shape=(
             jax.ShapeDtypeStruct((1, slide_width), BF16),
-            jax.ShapeDtypeStruct((rows, depth), BF16),
+            jax.ShapeDtypeStruct((rows, width), BF16),
         ),
         in_specs=[vmem, vmem, vmem, pl.BlockSpec(memory_space=pltpu.SMEM), vmem]
-        + [pl.BlockSpec(memory_space=pl.ANY)] * len(weights),
+        + [anywhere] * len(weights),
         out_specs=(vmem, vmem),
         scratch_shapes=[pltpu.VMEM(w.shape, BF16) for w in weights]
         + [pltpu.VMEM((n, chunk, width), BF16)] * 4
         + [
-            pltpu.VMEM((n, 8, 128), F32),
-            pltpu.VMEM((8, 128), F32),
-            pltpu.VMEM((n, 8, 128), F32),
+            pltpu.VMEM((1, width + slide_width), F32),
+            pltpu.VMEM((n, 1, width + slide_width), F32),
             pltpu.VMEM((REGION_SLOTS, hidden_units), F32),
             pltpu.VMEM((REGION_SLOTS, hidden_units), F32),
             dma((len(weights),)),
         ]
-        + [dma((n,))] * 8,
+        + [dma((n,))] * 6,
         compiler_params=pltpu.CompilerParams(
             collective_id=0, has_side_effects=True, vmem_limit_bytes=56 * 1024 * 1024
         ),
@@ -473,9 +483,30 @@
         tile_region.reshape(1, rows),
         slide_of_region.reshape(1, n),
         seg_offset,
-        ct,
+        slide_ct,
         *weights,
     )
+    return pl.pallas_call(
+        finish,
+        out_shape=(
+            jax.ShapeDtypeStruct((1, slide_width), BF16),
+            jax.ShapeDtypeStruct((rows, depth), BF16),
+        ),
+        in_specs=[anywhere] * 3,
+        out_specs=(vmem, anywhere),
+        scratch_shapes=[
+            pltpu.VMEM((rows, width), BF16),
+            pltpu.VMEM((depth // 512, 512, width), BF16),
+            pltpu.VMEM((depth // 512, rows, 512), BF16),
+            dma((2,)),
+            dma((depth // 512,)),
+            dma((depth // 512,)),
+        ],
+        compiler_params=pltpu.CompilerParams(vmem_limit_bytes=60 * 1024 * 1024),
+        cost_estimate=pl.CostEstimate(
+            flops=2 * rows * width * depth, bytes_accessed=2_000_000, transcendentals=0
+        ),
+    )(slide_row, returned, w_in)
 
 
 def solution(mesh):

time: 42.2 us -> 39.5 us (0.936)
  local copies, waits for them, and re-layouts: 3.01 us -> 0 us
  Pallas kernels: 37 us -> 38.7 us
  other arithmetic: 1.3 us -> 0 us
    pallas_call x0 -> x1, Pallas kernels: none -> 3.11 us  [local(): pl.pallas_call(finish, out_shape=(jax.ShapeDtypeStruct((1, slide_width),...]
    unnamed x2 -> x0, local copies, waits for them, and re-layouts: 3.01 us -> none
    pallas_call x1, Pallas kernels: 37 us -> 35.6 us  [local(): pl.pallas_call(functools.partial(kernel, n, chunk), out_shape=(jax.ShapeD...]
    unnamed x1 -> x0, other arithmetic: 0.71 us -> none
    pad x1 -> x0, other arithmetic: 0.6 us -> none  [local(): jnp.pad(slide_ct.astype(F32).reshape(slide_width // 128, 128), ((0, 8 - s...]
where the time goes in v2:
time: 39.5 us; the launch traced here: 39.4 us
  Pallas kernels  38.7 us (98%)
  between operations  0.64 us (2%)
    pallas_call x1, Pallas kernels, local(): pl.pallas_call(functools.partial(kernel, n, chunk), out_shape=(jax.ShapeD...  35.6 us
    pallas_call x1, Pallas kernels, local(): pl.pallas_call(finish, out_shape=(jax.ShapeDtypeStruct((1, slide_width),...  3.11 us

profile of v2, /device:TPU:0, one launch (start us, length us, event | category | flops | bytes accessed | tf_op | source)
XLA Modules:
  0.0 39.4 jit_solution(14462519796878835234)
XLA Ops:
  0.6 35.6 %shard_map.140 = (bf16[1,768]{1,0:T(2,128)(2,1)}, bf16[128,384]{1,0:T(8,128)(2,1)}) custom-call(bf16[128,1536]{1,0:T(8,128)(2,1)} %tiles_ref.1, s32[1,128]{1,0:T(1,128)} %bitcast.2, s32[1,16]{1,0:T(1,128)} %bitcast.3, s32[12]{0:T(128)} %offset_ref.1, bf16[1,768]{1,0:T(2,128)(2,1)} %ct_ref.1, bf16[1536,384]{1,0:T(8,128)(2,1)} %w_in_hbm.3, ...), custom_call_target="tpu_custom_call" | custom-call | flops 2000000000 | bytes 12000000 | tf_op jit(solution)/shard_map/pallas_call | solution.py:456
  36.3 3.1 %shard_map.141 = (bf16[1,768]{1,0:T(2,128)(2,1)}, bf16[128,1536]{1,0:T(8,128)(2,1)}) custom-call(bf16[1,768]{1,0:T(2,128)(2,1)} %get-tuple-element.4.slide_hbm, bf16[128,384]{1,0:T(8,128)(2,1)} %get-tuple-element.5.returned_hbm, bf16[1536,384]{1,0:T(8,128)(2,1)} %w_in_hbm.3), custom_call_target="tpu_custom_call" | custom-call | flops 150994944 | bytes 2000000 | tf_op jit(solution)/shard_map/pallas_call | solution.py:489

commit v3 on v2

--- a/solution.py
+++ b/solution.py
@@ -62,11 +62,11 @@
 def kernel(
     n,
     chunk,
-    tiles_ref,
-    region_ref,
+    tiles_hbm,
+    region_hbm,
     slides_ref,
     offset_ref,
-    ct_ref,
+    ct_hbm,
     w_in_hbm,
     w_qkv_hbm,
     w_attn_out_hbm,
@@ -75,8 +75,10 @@
     w_slide_in_hbm,
     w_slide_qkv_hbm,
     w_slide_out_hbm,
-    slide_out_ref,
     returned_ref,
+    tiles_ref,
+    region_ref,
+    ct_ref,
     w_in,
     w_qkv,
     w_attn_out,
@@ -93,7 +95,10 @@
     pool_all,
     up_out,
     up_slope,
+    allowed_ref,
+    turned_ref,
     w_sem,
+    in_sem,
     x_send_sem,
     x_recv_sem,
     g_send_sem,
@@ -113,8 +118,14 @@
         )
         return carry
 
-    lax.fori_loop(1, n, greet, 0)
-
+    early = [
+        pltpu.make_async_copy(source, target, in_sem.at[i])
+        for i, (source, target) in enumerate(
+            [(tiles_hbm, tiles_ref), (region_hbm, region_ref), (ct_hbm, ct_ref)]
+        )
+    ]
+    for load in early:
+        load.start()
     loads = [
         pltpu.make_async_copy(source, target, w_sem.at[i])
         for i, (source, target) in enumerate(
@@ -132,11 +143,13 @@
     ]
     for load in loads:
         load.start()
+    lax.fori_loop(1, n, greet, 0)
 
     rows, width = tiles_ref.shape[0], w_in.shape[1]
     slots_sent = n * chunk
     capacity = REGION_SLOTS // n
 
+    early[1].wait()
     region = region_ref[...]
     named = (iota((n, rows), 0) == region).astype(F32)
     earlier = (iota((rows, rows), 0) < iota((rows, rows), 1)).astype(BF16)
@@ -174,6 +187,7 @@
             device_id_type=MESH,
         )
 
+    early[0].wait()
     loads[0].wait()
     projected = mm(tiles_ref[...], w_in[...]).astype(BF16)
     outgoing = jnp.where(held, mm(place, projected), EMPTY).astype(BF16)
@@ -187,6 +201,7 @@
     everyone(start_x)
 
     recv_x[me] = send_x[me]
+    early[2].wait()
     pool_own[:, width:] = ct_ref[...].astype(F32)
     square = iota((rows, rows), 0) == iota((rows, rows), 1)
     target_col = jnp.sum(jnp.where(square, target, 0.0), axis=1, keepdims=True)
@@ -197,6 +212,20 @@
             iota((REGION_SLOTS, slots_sent), 1) == slot // capacity * chunk + slot % capacity
         ).astype(BF16)
 
+    slides_row = slides_ref[...]
+    own = iota((n, n), 0) == iota((n, n), 1)
+    slides_col = jnp.sum(jnp.where(own, slides_row, 0), axis=1, keepdims=True)
+    same = slides_col == slides_row
+    key_index = iota((n, n), 1)
+    allowed_ref[...] = jnp.concatenate(
+        [
+            jnp.where(
+                same & ((lax.rem(key_index + offset_ref[h], DILATION) == 0) | own), 1.0, 0.0
+            )
+            for h in range(HEADS_S)
+        ],
+        axis=0,
+    )
     for load in loads[1:5]:
         load.wait()
 
@@ -266,6 +295,8 @@
     everyone(start_pool)
     pool_all[me] = pool_own[...]
 
+    for h in range(HEADS_R):
+        turned_ref[h] = weights[h].astype(BF16).T
     for c in range(0, hidden_units, block):
         u = up_out[:, c : c + block]
         bent = up_slope[:, c : c + block]
@@ -308,30 +339,19 @@
             total = term if total is None else total + term
         return total
 
-    slides_row = slides_ref[...]
-    own = iota((n, n), 0) == iota((n, n), 1)
-    slides_col = jnp.sum(jnp.where(own, slides_row, 0), axis=1, keepdims=True)
-    same = slides_col == slides_row
-    key_index = iota((n, n), 1)
-    allowed = jnp.concatenate(
-        [
-            jnp.where(
-                same & ((lax.rem(key_index + offset_ref[h], DILATION) == 0) | own), 1.0, 0.0
-            )
-            for h in range(HEADS_S)
-        ],
-        axis=0,
-    )
     sq_heads = spread(sq)
     slide_scores = mm_nt(sq_heads, sk) * slide_factor
-    slide_weights = softmax(jnp.where(allowed > 0, slide_scores, -1e30))
+    slide_weights = softmax(jnp.where(allowed_ref[...] > 0, slide_scores, -1e30))
     slide_rounded = slide_weights.astype(BF16)
     slide_mixed = gather(mm(slide_rounded, sv)).astype(BF16)
     slide_out = token + mm(slide_mixed, w_slide_out[...])
     mine = iota((n, 1), 0) == me
-    slide_out_ref[...] = jnp.sum(
-        jnp.where(mine, slide_out, 0.0), axis=0, keepdims=True
-    ).astype(BF16)
+    slide_row = jnp.sum(jnp.where(mine, slide_out, 0.0), axis=0, keepdims=True)
+    slide_block = jnp.zeros((16, width), F32)
+    for i in range(slide_width // width):
+        part = slide_row[:, i * width : i * width + width]
+        slide_block = jnp.where(iota((16, 1), 0) == i, part, slide_block)
+    returned_ref[rows : rows + 16, :] = slide_block.astype(BF16)
 
     g_mixed = mm_nt(ct.astype(BF16), w_slide_out[...]).astype(BF16).astype(F32)
     g_heads = spread(g_mixed)
@@ -368,7 +388,7 @@
             q_h = jnp.where(lane == h, q, nothing)
             k_h = jnp.where(lane == h, k, nothing)
             g_s = (softmax_back(chances, mm_nt(g_h, v)) * factor).astype(BF16)
-            terms = (mm(g_s, k_h), mm_tn(g_s, q_h), mm_tn(chances.astype(BF16), g_h))
+            terms = (mm(g_s, k_h), mm_tn(g_s, q_h), mm(turned_ref[pair * per + h], g_h))
             sums = terms if sums is None else tuple(a + b for a, b in zip(sums, terms))
         g_qs.append(sums[0])
         g_ks.append(sums[1])
@@ -396,7 +416,7 @@
         arrival(send_g.at[peer], recv_g, g_send_sem, g_recv_sem, peer).wait_recv()
 
     everyone(wait_g)
-    returned_ref[...] = mm(fetch, recv_g[...].reshape(slots_sent, width)).astype(BF16)
+    returned_ref[:rows, :] = mm(fetch, recv_g[...].reshape(slots_sent, width)).astype(BF16)
 
     def wait_g_sent(peer):
         exchange(send_g.at[peer], recv_g, g_send_sem, g_recv_sem, peer).wait_send()
@@ -404,29 +424,12 @@
     everyone(wait_g_sent)
 
 
-def finish(
-    slide_hbm, returned_hbm, w_in_hbm, slide_out_ref, grad_hbm, returned, w_in, grad, sem, w_sem, out_sem
-):
-    blocks = range(grad.shape[0])
-    slide_copy = pltpu.make_async_copy(slide_hbm, slide_out_ref, sem.at[0])
-    returned_copy = pltpu.make_async_copy(returned_hbm, returned, sem.at[1])
-    loads = [pltpu.make_async_copy(w_in_hbm.at[i * 512 : i * 512 + 512], w_in.at[i], w_sem.at[i]) for i in blocks]
-    returned_copy.start()
-    for load in loads:
-        load.start()
-    slide_copy.start()
-    returned_copy.wait()
-    copies = []
-    for i in blocks:
-        loads[i].wait()
-        grad[i] = mm_nt(returned[...], w_in[i]).astype(BF16)
-        copies.append(
-            pltpu.make_async_copy(grad.at[i], grad_hbm.at[:, i * 512 : i * 512 + 512], out_sem.at[i])
-        )
-        copies[i].start()
-    slide_copy.wait()
-    for copy in copies:
-        copy.wait()
+def finish(returned_ref, w_in_ref, slide_out_ref, grad_ref):
+    rows, width = grad_ref.shape[0], returned_ref.shape[1]
+    slide_rows = returned_ref[rows : rows + 16, :].astype(F32)
+    for i in range(slide_out_ref.shape[1] // width):
+        slide_out_ref[:, i * width : i * width + width] = slide_rows[i : i + 1].astype(BF16)
+    grad_ref[...] = mm_nt(returned_ref[:rows, :], w_in_ref[...]).astype(BF16)
 
 
 def local(
@@ -453,23 +456,28 @@
     vmem = pl.BlockSpec(memory_space=pltpu.VMEM)
     anywhere = pl.BlockSpec(memory_space=pl.ANY)
     dma = pltpu.SemaphoreType.DMA
-    slide_row, returned = pl.pallas_call(
+    returned = pl.pallas_call(
         functools.partial(kernel, n, chunk),
-        out_shape=(
-            jax.ShapeDtypeStruct((1, slide_width), BF16),
-            jax.ShapeDtypeStruct((rows, width), BF16),
-        ),
-        in_specs=[vmem, vmem, vmem, pl.BlockSpec(memory_space=pltpu.SMEM), vmem]
+        out_shape=jax.ShapeDtypeStruct((rows + 16, width), BF16),
+        in_specs=[anywhere, anywhere, vmem, pl.BlockSpec(memory_space=pltpu.SMEM), anywhere]
         + [anywhere] * len(weights),
-        out_specs=(vmem, vmem),
-        scratch_shapes=[pltpu.VMEM(w.shape, BF16) for w in weights]
+        out_specs=vmem,
+        scratch_shapes=[
+            pltpu.VMEM((rows, depth), BF16),
+            pltpu.VMEM((1, rows), jnp.int32),
+            pltpu.VMEM((1, slide_width), BF16),
+        ]
+        + [pltpu.VMEM(w.shape, BF16) for w in weights]
         + [pltpu.VMEM((n, chunk, width), BF16)] * 4
         + [
             pltpu.VMEM((1, width + slide_width), F32),
             pltpu.VMEM((n, 1, width + slide_width), F32),
             pltpu.VMEM((REGION_SLOTS, hidden_units), F32),
             pltpu.VMEM((REGION_SLOTS, hidden_units), F32),
+            pltpu.VMEM((HEADS_S * n, n), F32),
+            pltpu.VMEM((HEADS_R, REGION_SLOTS, REGION_SLOTS), BF16),
             dma((len(weights),)),
+            dma((3,)),
         ]
         + [dma((n,))] * 6,
         compiler_params=pltpu.CompilerParams(
@@ -492,21 +500,13 @@
             jax.ShapeDtypeStruct((1, slide_width), BF16),
             jax.ShapeDtypeStruct((rows, depth), BF16),
         ),
-        in_specs=[anywhere] * 3,
-        out_specs=(vmem, anywhere),
-        scratch_shapes=[
-            pltpu.VMEM((rows, width), BF16),
-            pltpu.VMEM((depth // 512, 512, width), BF16),
-            pltpu.VMEM((depth // 512, rows, 512), BF16),
-            dma((2,)),
-            dma((depth // 512,)),
-            dma((depth // 512,)),
-        ],
-        compiler_params=pltpu.CompilerParams(vmem_limit_bytes=60 * 1024 * 1024),
+        in_specs=[vmem, vmem],
+        out_specs=(vmem, vmem),
+        compiler_params=pltpu.CompilerParams(vmem_limit_bytes=16 * 1024 * 1024),
         cost_estimate=pl.CostEstimate(
             flops=2 * rows * width * depth, bytes_accessed=2_000_000, transcendentals=0
         ),
-    )(slide_row, returned, w_in)
+    )(returned, w_in)
 
 
 def solution(mesh):

time: 39.5 us -> 38 us (0.962)
  Pallas kernels: 38.7 us -> 36.1 us
  local copies, waits for them, and re-layouts: 0 us -> 0.89 us
    pallas_call x1, Pallas kernels: 3.11 us -> 1.25 us  [local(): pl.pallas_call(finish, out_shape=(jax.ShapeDtypeStruct((1, slide_width),...]
    unnamed x0 -> x4, local copies, waits for them, and re-layouts: none -> 0.89 us
    pallas_call x1, Pallas kernels: 35.6 us -> 34.8 us  [local(): pl.pallas_call(functools.partial(kernel, n, chunk), out_shape=jax.ShapeDt...]
where the time goes in v3:
time: 38 us; the launch traced here: 37.6 us
  Pallas kernels  36.1 us (95%)
  local copies, waits for them, and re-layouts  0.89 us (2%)
  between operations  0.67 us (2%)
    pallas_call x1, Pallas kernels, local(): pl.pallas_call(functools.partial(kernel, n, chunk), out_shape=jax.ShapeDt...  34.8 us
    pallas_call x1, Pallas kernels, local(): pl.pallas_call(finish, out_shape=(jax.ShapeDtypeStruct((1, slide_width),...  1.25 us
    unnamed x4, local copies, waits for them, and re-layouts  0.89 us

profile of v3, /device:TPU:0, one launch (start us, length us, event | category | flops | bytes accessed | tf_op | source)
XLA Modules:
  0.0 37.6 jit_solution(17764155320037882652)
XLA Ops:
  0.6 0.0 copy-start
  0.6 34.8 %shard_map.140.returned_ref = bf16[144,384]{1,0:T(8,128)(2,1)} custom-call(bf16[128,1536]{1,0:T(8,128)(2,1)} %tiles_hbm.1, s32[1,128]{1,0:T(1,128)} %bitcast.2, s32[1,16]{1,0:T(1,128)} %bitcast.3, s32[12]{0:T(128)} %offset_ref.1, bf16[1,768]{1,0:T(2,128)(2,1)} %ct_hbm.1, bf16[1536,384]{1,0:T(8,128)(2,1)} %w_in_ref.1, bf16[384,1152]{1,0:T(8,128)(2,1)} %w_qkv_hbm.1, ...), custom_call_target="tpu_custom_call" | custom-call | flops 2000000000 | bytes 12000000 | tf_op jit(solution)/shard_map/pallas_call | solution.py:459
  35.5 0.0 copy-done
  35.5 0.0 copy-start.1
  35.5 0.9 %copy-done.1 = bf16[144,384]{1,0:T(8,128)(2,1)S(1)} copy-done((bf16[144,384]{1,0:T(8,128)(2,1)S(1)}, bf16[144,384]{1,0:T(8,128)(2,1)}, u32[]{:S(2)}) %copy-start.1) | copy-done | bytes 110616
  36.4 1.2 %shard_map.141 = (bf16[1,768]{1,0:T(2,128)(2,1)}, bf16[128,1536]{1,0:T(8,128)(2,1)}) custom-call(bf16[144,384]{1,0:T(8,128)(2,1)S(1)} %copy-done.1, bf16[1536,384]{1,0:T(8,128)(2,1)S(1)} %copy-done), custom_call_target="tpu_custom_call" | custom-call | flops 150994944 | bytes 2000000 | tf_op jit(solution)/shard_map/pallas_call | solution.py:497
Async XLA Ops:
  0.6 34.8 %copy-start = (bf16[1536,384]{1,0:T(8,128)(2,1)S(1)}, bf16[1536,384]{1,0:T(8,128)(2,1)}, u32[]{:S(2)}) copy-start(bf16[1536,384]{1,0:T(8,128)(2,1)} %w_in_ref.1) | copy-start | bytes 3538948
  35.5 0.9 %copy-start.1 = (bf16[144,384]{1,0:T(8,128)(2,1)S(1)}, bf16[144,384]{1,0:T(8,128)(2,1)}, u32[]{:S(2)}) copy-start(bf16[144,384]{1,0:T(8,128)(2,1)} %shard_map.140.returned_ref) | copy-start | bytes 331780
